TPU v7x, 32 devices: a whole 2x2x4 slice. The times are simulated.
32 devices in a mesh: bins: 8 (over y, x, core), slab: 4 (over z).
Axes of the slice: x: 2, y: 2, z: 4, core: 2. Of those that a mesh axis runs over, the one named last changes fastest.
Arguments:
- free_velocity: float32 [6, 262144], P(None, ('bins', 'slab')), may hold values from -9 to 9
- inverse_mass: float32 [6, 262144], P(None, ('bins', 'slab')), may hold values from 0.5 to 2
- first_body: int32 [131072], P(('bins', 'slab')), may hold values from 0 to 8191
- second_body: int32 [131072], P(('bins', 'slab')), may hold values from 0 to 20479
- send_list: int32 [8, 49152], P(None, ('bins', 'slab')), may hold values from 0 to 8191
- jacobian: float32 [2, 3, 6, 131072], P(None, None, None, ('bins', 'slab')), may hold values from -2.5 to 2.5
- contact_bias: float32 [3, 131072], P(None, ('bins', 'slab')), may hold values from -27 to 27
- compliance: float32 [131072], P(('bins', 'slab')), may hold values from 0.05 to 0.5
- friction: float32 [131072], P(('bins', 'slab')), may hold values from 0.2 to 0.9
- warm_start: float32 [3, 131072], P(None, ('bins', 'slab')), may hold values from -4.5 to 4.5
Outputs:
- impulses: float32 [3, 131072], P(None, ('bins', 'slab'))
- velocity: float32 [6, 262144], P(None, ('bins', 'slab'))
All inputs are finite; a program needn't handle non-finite values.
Results may differ from a plain program's by a relative error of at most 0.0003.
Values sent between devices are 32-bit elements; how exact they have to be, the bound alone decides.
A program may use at most 128 MiB of HBM per device.

v0:
```python
import math

import jax
import jax.numpy as jnp
from jax import lax
from jax.sharding import PartitionSpec as P

ITERS = 3


bin_steps = (-1, -1, -1, 0, 0, 1, 1, 1)
slab_steps = (-1, 0, 1, -1, 1, -1, 0, 1)
SAFETY = 0.3
TINY = 1e-06
FLOOR = 1e-20


def padded(shard, sides, width):
    for axis, dim in sides:
        size, length = (lax.axis_size(axis), shard.shape[dim])
        up = [(i, (i + 1) % size) for i in range(size - 1)]
        down = [(j, i) for i, j in up]
        last = lax.slice_in_dim(shard, length - width, length, axis=dim)
        initial = lax.slice_in_dim(shard, 0, width, axis=dim)
        before = lax.ppermute(last, axis, up)
        after = lax.ppermute(initial, axis, down)
        shard = jnp.concatenate([before, shard, after], axis=dim)
    return shard


def momentum_table(steps_count):
    theta_now = 1.0
    momentum = []
    for iteration in range(steps_count):
        theta_next = (
            -theta_now * theta_now + theta_now * math.sqrt(theta_now * theta_now + 4.0)
        ) / 2.0
        momentum.append(theta_now * (1.0 - theta_now) / (theta_now * theta_now + theta_next))
        theta_now = theta_next
    return momentum


def project(values, friction):
    normal = values[0]
    tangent_one = values[1]
    tangent_two = values[2]
    magnitude = jnp.sqrt(tangent_one * tangent_one + tangent_two * tangent_two)
    projected = jnp.maximum(friction * magnitude + normal, 0.0) / (friction * friction + 1.0)
    inside = magnitude <= friction * normal
    normal_new = jnp.where(inside, normal, projected)
    tangent_limit = friction * normal_new
    factor = tangent_limit / jnp.maximum(jnp.maximum(magnitude, tangent_limit), FLOOR)
    return jnp.stack([normal_new, tangent_one * factor, tangent_two * factor])


def rim_place(payload):
    blank = jnp.zeros_like(payload[:, 0])
    blocks_grid = [[blank, blank, blank], [blank, blank, blank], [blank, blank, blank]]
    for direction in range(8):
        blocks_grid[1 + bin_steps[direction]][1 + slab_steps[direction]] = payload[:, direction]
    return jnp.stack([jnp.stack(grid_row) for grid_row in blocks_grid])


def rim_take(extended):
    gathered = [
        extended[2 + 2 * bin_steps[direction], 2 + 2 * slab_steps[direction]]
        for direction in range(8)
    ]
    return jnp.stack(gathered, axis=1)


def pull(payload):
    placed = rim_place(payload)
    extended = padded(placed, (("bins", 0), ("slab", 1)), 1)
    return rim_take(extended)


def push(payload):
    placed = rim_place(payload)
    extended = padded(placed, (("bins", 0), ("slab", 1)), 1)
    return rim_take(extended)


def shards(
    free_velocity,
    inverse_mass,
    first_body,
    second_body,
    send_list,
    jacobian,
    contact_bias,
    compliance,
    friction,
    warm_start,
):
    bodies = free_velocity.shape[1]
    halo_width = send_list.shape[1]
    contacts_total = 3.0 * first_body.shape[0] * lax.axis_size("bins") * lax.axis_size("slab")
    first_blocks = jacobian[0]
    second_blocks = jacobian[1]
    flat_list = send_list.reshape(-1)

    def spread(multipliers):
        first_terms = (
            first_blocks[0] * multipliers[0]
            + first_blocks[1] * multipliers[1]
            + first_blocks[2] * multipliers[2]
        )
        second_terms = (
            second_blocks[0] * multipliers[0]
            + second_blocks[1] * multipliers[1]
            + second_blocks[2] * multipliers[2]
        )
        accumulator = jnp.zeros((6, bodies + 8 * halo_width), jnp.float32)
        accumulator = accumulator.at[:, first_body].add(first_terms)
        accumulator = accumulator.at[:, second_body].add(second_terms)
        outgoing = accumulator[:, bodies:].reshape(6, 8, halo_width)
        incoming = push(outgoing)
        return accumulator[:, :bodies].at[:, flat_list].add(incoming.reshape(6, 8 * halo_width))

    momentum = momentum_table(ITERS)
    previous_point = jnp.zeros_like(warm_start)
    previous_forces = jnp.zeros_like(free_velocity)
    impulses = warm_start
    extrapolated = warm_start
    for iteration in range(ITERS):
        current = spread(extrapolated)
        change = extrapolated - previous_point
        force_change = current - previous_forces
        partial_squares = jnp.sum(change * change)
        partial_curve = jnp.sum(inverse_mass * force_change * force_change) + jnp.sum(
            compliance * change * change
        )
        total_squares, total_curve = lax.psum((partial_squares, partial_curve), ("bins", "slab"))
        stepsize = (
            SAFETY * (total_squares / contacts_total + TINY) / (total_curve / contacts_total + TINY)
        )
        velocity = free_velocity + inverse_mass * current
        gradient_outgoing = velocity[:, flat_list].reshape(6, 8, halo_width)
        gradient_incoming = pull(gradient_outgoing)
        extended = jnp.concatenate([velocity, gradient_incoming.reshape(6, 8 * halo_width)], axis=1)
        first_speed = extended[:, first_body]
        second_speed = extended[:, second_body]
        result = contact_bias + compliance * extrapolated
        for column in range(6):
            result = (
                result
                + first_blocks[:, column] * first_speed[column]
                + second_blocks[:, column] * second_speed[column]
            )
        updated = project(extrapolated - stepsize * result, friction)
        previous_point = extrapolated
        previous_forces = current
        extrapolated = updated + momentum[iteration] * (updated - impulses)
        impulses = updated
    final_forces = spread(impulses)
    return (impulses, free_velocity + inverse_mass * final_forces)


def solution(mesh):
    return jax.shard_map(
        shards,
        mesh=mesh,
        in_specs=(
            P(None, ("bins", "slab")),
            P(None, ("bins", "slab")),
            P(("bins", "slab")),
            P(("bins", "slab")),
            P(None, ("bins", "slab")),
            P(None, None, None, ("bins", "slab")),
            P(None, ("bins", "slab")),
            P(("bins", "slab")),
            P(("bins", "slab")),
            P(None, ("bins", "slab")),
        ),
        out_specs=(P(None, ("bins", "slab")), P(None, ("bins", "slab"))),
        check_vma=False,
    )
```

profile of v0, /device:TPU:0, one launch (start us, length us, event | category | flops | bytes accessed | tf_op | source)
XLA Modules:
  0.0 1258.0 jit_solution(10640791638589136899)
XLA Ops:
  7.4 27.3 %scatter_custom_fusion = f32[6,20480]{0,1:T(8,128)} fusion(s32[4096]{0:T(1024)S(1)} %get-tuple-element.229, f32[4096,6]{1,0:T(8,128)} %copy.338, f32[]{:T(128)} %constant.10.clone.1), kind=kCustom, calls=%fused_computation.30 | custom fusion | flops 24576 | bytes 492032 | tf_op jit(solution)/shard_map/scatter-add | solution.py:115
  34.7 28.1 %scatter_fusion = f32[6,20480]{0,1:T(8,128)} fusion(f32[6,20480]{0,1:T(8,128)} %scatter_custom_fusion, s32[4096]{0:T(1024)S(1)} %get-tuple-element.226, f32[4096,6]{1,0:T(8,128)S(1)} %copy.342), kind=kCustom, calls=%fused_computation.10 | custom fusion | flops 24576 | bytes 311296 | tf_op jit(solution)/shard_map/scatter-add | solution.py:116
  111.0 63.5 %scatter_fusion.1 = f32[6,8192]{0,1:T(8,128)} fusion(f32[6,8192]{0,1:T(8,128)} %slice.913, s32[12288]{0:T(1024)S(1)} %bitcast.568, f32[12288,6]{1,0:T(8,128)} %bitcast.564), kind=kCustom, calls=%fused_computation.11 | custom fusion | flops 73728 | bytes 933888 | tf_op jit(solution)/shard_map/scatter-add | solution.py:119
  180.8 43.5 %gather_fusion = f32[12288,6]{1,0:T(8,128)} fusion(f32[6,8192]{0,1:T(8,128)} %copy.377, s32[12288]{0:T(1024)S(1)} %broadcast_clamp_fusion), kind=kCustom, calls=%fused_computation | custom fusion | bytes 638976 | tf_op jit(solution)/shard_map/gather | solution.py:139
  243.4 42.4 %all-reduce.2 = (f32[]{:T(128)}, f32[]{:T(128)}) all-reduce(f32[]{:T(128)} %get-tuple-element.53, f32[]{:T(128)S(6)} %add.311), channel_id=1, replica_groups=mesh['bins'=8,'slab'=4] {'bins','slab'}, use_global_device_ids=true, to_apply=%region_1.0 | all-reduce | flops 2 | bytes 16 | tf_op jit(solution)/shard_map/psum | solution.py:134
  305.1 10.6 pad_maximum_fusion
  315.7 16.7 %gather_fusion.1 = f32[4096,6]{1,0:T(8,128)S(1)} fusion(f32[6,20480]{0,1:T(8,128)} %pad_maximum_fusion, s32[4096]{0:T(1024)} %get-tuple-element.230), kind=kCustom, calls=%fused_computation.1 | custom fusion | bytes 212992 | tf_op jit(solution)/shard_map/gather | solution.py:142
  332.5 6.6 slice_reduce_fusion.35
  339.1 16.9 %gather_fusion.2 = f32[4096,6]{1,0:T(8,128)S(1)} fusion(f32[6,20480]{0,1:T(8,128)} %pad_maximum_fusion, s32[4096]{0:T(1024)} %get-tuple-element.225), kind=kCustom, calls=%fused_computation.2 | custom fusion | bytes 212992 | tf_op jit(solution)/shard_map/gather | solution.py:143
  356.2 6.0 slice_reduce_fusion.34
  366.1 27.1 %scatter_custom_fusion.3 = f32[6,20480]{0,1:T(8,128)} fusion(s32[4096]{0:T(1024)} %copy-done.91, f32[4096,6]{1,0:T(8,128)S(1)} %copy.379, f32[]{:T(128)} %constant.10.clone.1), kind=kCustom, calls=%fused_computation.28 | custom fusion | flops 24576 | bytes 492032 | tf_op jit(solution)/shard_map/scatter-add | solution.py:115
  394.8 28.2 %scatter_fusion.2 = f32[6,20480]{0,1:T(8,128)} fusion(f32[6,20480]{0,1:T(8,128)} %scatter_custom_fusion.3, s32[4096]{0:T(1024)} %copy-done.57, f32[4096,6]{1,0:T(8,128)S(1)} %copy.380), kind=kCustom, calls=%fused_computation.13 | custom fusion | flops 24576 | bytes 311296 | tf_op jit(solution)/shard_map/scatter-add | solution.py:116
  467.4 63.6 %scatter_fusion.3 = f32[6,8192]{0,1:T(8,128)} fusion(f32[6,8192]{0,1:T(8,128)} %slice.981, s32[12288]{0:T(1024)S(1)} %bitcast.569, f32[12288,6]{1,0:T(8,128)} %bitcast.565), kind=kCustom, calls=%fused_computation.14 | custom fusion | flops 73728 | bytes 933888 | tf_op jit(solution)/shard_map/scatter-add | solution.py:119
  537.1 43.5 %gather_fusion.3 = f32[12288,6]{1,0:T(8,128)} fusion(f32[6,8192]{0,1:T(8,128)} %copy.415, s32[12288]{0:T(1024)S(1)} %copy-done.34), kind=kCustom, calls=%fused_computation.3 | custom fusion | bytes 638976 | tf_op jit(solution)/shard_map/gather | solution.py:139
  601.1 41.8 %all-reduce.1 = (f32[]{:T(128)}, f32[]{:T(128)}) all-reduce(f32[]{:T(128)} %get-tuple-element.51, f32[]{:T(128)S(6)} %add.336), channel_id=1, replica_groups=mesh['bins'=8,'slab'=4] {'bins','slab'}, use_global_device_ids=true, to_apply=%region_9.10 | all-reduce | flops 2 | bytes 16 | tf_op jit(solution)/shard_map/psum | solution.py:134
  662.2 10.6 pad_maximum_fusion.1
  672.8 18.1 %gather_fusion.4 = f32[4096,6]{1,0:T(8,128)} fusion(f32[6,20480]{0,1:T(8,128)} %pad_maximum_fusion.1, s32[4096]{0:T(1024)S(1)} %copy-done.60), kind=kCustom, calls=%fused_computation.4 | custom fusion | bytes 212992 | tf_op jit(solution)/shard_map/gather | solution.py:142
  691.0 16.9 %gather_fusion.5 = f32[4096,6]{1,0:T(8,128)S(1)} fusion(f32[6,20480]{0,1:T(8,128)} %pad_maximum_fusion.1, s32[4096]{0:T(1024)} %get-tuple-element.225), kind=kCustom, calls=%fused_computation.5 | custom fusion | bytes 212992 | tf_op jit(solution)/shard_map/gather | solution.py:143
  707.8 11.4 slice_reduce_fusion.23
  729.3 27.5 %scatter_custom_fusion.6 = f32[6,20480]{0,1:T(8,128)} fusion(s32[4096]{0:T(1024)} %copy-done.91, f32[4096,6]{1,0:T(8,128)S(1)} %copy.416, f32[]{:T(128)} %constant.10.clone.1), kind=kCustom, calls=%fused_computation.26 | custom fusion | flops 24576 | bytes 492032 | tf_op jit(solution)/shard_map/scatter-add | solution.py:115
  758.3 28.2 %scatter_fusion.4 = f32[6,20480]{0,1:T(8,128)} fusion(f32[6,20480]{0,1:T(8,128)} %scatter_custom_fusion.6, s32[4096]{0:T(1024)} %copy-done.57, f32[4096,6]{1,0:T(8,128)S(1)} %copy.417), kind=kCustom, calls=%fused_computation.16 | custom fusion | flops 24576 | bytes 311296 | tf_op jit(solution)/shard_map/scatter-add | solution.py:116
  830.5 63.6 %scatter_fusion.5 = f32[6,8192]{0,1:T(8,128)} fusion(f32[6,8192]{0,1:T(8,128)} %slice.1037, s32[12288]{0:T(1024)S(1)} %bitcast.570, f32[12288,6]{1,0:T(8,128)} %bitcast.566), kind=kCustom, calls=%fused_computation.17 | custom fusion | flops 73728 | bytes 933888 | tf_op jit(solution)/shard_map/scatter-add | solution.py:119
  900.3 43.5 %gather_fusion.6 = f32[12288,6]{1,0:T(8,128)} fusion(f32[6,8192]{0,1:T(8,128)} %copy.452, s32[12288]{0:T(1024)S(1)} %copy-done.35), kind=kCustom, calls=%fused_computation.6 | custom fusion | bytes 638976 | tf_op jit(solution)/shard_map/gather | solution.py:139
  963.0 42.9 %all-reduce = (f32[]{:T(128)}, f32[]{:T(128)}) all-reduce(f32[]{:T(128)} %get-tuple-element.49, f32[]{:T(128)S(6)} %add.360), channel_id=1, replica_groups=mesh['bins'=8,'slab'=4] {'bins','slab'}, use_global_device_ids=true, to_apply=%region_17.18 | all-reduce | flops 2 | bytes 16 | tf_op jit(solution)/shard_map/psum | solution.py:134
  1024.5 10.6 pad_maximum_fusion.2
  1035.1 18.1 %gather_fusion.7 = f32[4096,6]{1,0:T(8,128)} fusion(f32[6,20480]{0,1:T(8,128)} %pad_maximum_fusion.2, s32[4096]{0:T(1024)S(1)} %copy-done.61), kind=kCustom, calls=%fused_computation.7 | custom fusion | bytes 212992 | tf_op jit(solution)/shard_map/gather | solution.py:142
  1053.3 14.9 %gather_fusion.8 = f32[4096,6]{1,0:T(8,128)S(1)} fusion(f32[6,20480]{0,1:T(8,128)} %pad_maximum_fusion.2, s32[4096]{0:T(1024)S(1)} %copy-done.59), kind=kCustom, calls=%fused_computation.8 | custom fusion | bytes 212992 | tf_op jit(solution)/shard_map/gather | solution.py:143
  1068.2 11.4 slice_reduce_fusion.11
  1087.1 27.3 %scatter_custom_fusion.9 = f32[6,20480]{0,1:T(8,128)} fusion(s32[4096]{0:T(1024)} %copy-done.91, f32[4096,6]{1,0:T(8,128)S(1)} %copy.453, f32[]{:T(128)} %constant.10.clone.1), kind=kCustom, calls=%fused_computation.24 | custom fusion | flops 24576 | bytes 492032 | tf_op jit(solution)/shard_map/scatter-add | solution.py:115
  1115.1 28.1 %scatter_fusion.6 = f32[6,20480]{0,1:T(8,128)} fusion(f32[6,20480]{0,1:T(8,128)} %scatter_custom_fusion.9, s32[4096]{0:T(1024)S(1)} %copy-done.58, f32[4096,6]{1,0:T(8,128)S(1)} %copy.454), kind=kCustom, calls=%fused_computation.19 | custom fusion | flops 24576 | bytes 311296 | tf_op jit(solution)/shard_map/scatter-add | solution.py:116
  1183.5 63.5 %scatter_fusion.7 = f32[6,8192]{0,1:T(8,128)} fusion(f32[6,8192]{0,1:T(8,128)} %slice.1090, s32[12288]{0:T(1024)S(1)} %bitcast.571, f32[12288,6]{1,0:T(8,128)} %bitcast.563), kind=kCustom, calls=%fused_computation.20 | custom fusion | flops 73728 | bytes 933888 | tf_op jit(solution)/shard_map/scatter-add | solution.py:119
  1247.1 7.2 multiply_add_fusion
  (487 shorter events, 337.7 us)
Async XLA Ops:
  72.7 20.9 %collective-permute-start = (f32[1,3,6,1536]{3,0,2,1:T(1,128)}, f32[1,3,6,1536]{3,0,2,1:T(1,128)}, u32[]{:S(2)}, u32[]{:S(2)}) collective-permute-start(f32[1,3,6,1536]{3,0,2,1:T(1,128)} %stack.184), channel_id=1, source_target_pairs={{0,4},{4,8},{8,12},{12,16},{16,20},{20,24},{24,28},{1,5},{5,9},{9,... | collective-permute-start | bytes 331784 | tf_op jit(solution)/shard_map/ppermute | solution.py:25
  78.4 16.4 %collective-permute-start.1 = (f32[1,3,6,1536]{3,0,2,1:T(1,128)}, f32[1,3,6,1536]{3,0,2,1:T(1,128)}, u32[]{:S(2)}, u32[]{:S(2)}) collective-permute-start(f32[1,3,6,1536]{3,0,2,1:T(1,128)} %stack.186), channel_id=1, source_target_pairs={{4,0},{8,4},{12,8},{16,12},{20,16},{24,20},{28,24},{5,1},{9,5},{13... | collective-permute-start | bytes 331784 | tf_op jit(solution)/shard_map/ppermute | solution.py:26
  87.0 93.7 %copy-start.33 = (s32[12288]{0:T(1024)}, s32[12288]{0:T(1024)S(1)}, u32[]{:S(2)}) copy-start(s32[12288]{0:T(1024)S(1)} %broadcast_clamp_fusion) | copy-start | bytes 147460
  92.5 198.1 %copy-start.85 = (f32[3]{0:T(128)}, f32[3]{0:T(128)S(1)}, u32[]{:S(2)}) copy-start(f32[3]{0:T(128)S(1)} %pad.70.clone) | copy-start | bytes 40
  96.0 8.5 collective-permute-start.3
  97.5 9.0 collective-permute-start.2
  238.5 51.2 %collective-permute-start.4 = (f32[1,3,6,1536]{3,0,2,1:T(1,128)}, f32[1,3,6,1536]{3,0,2,1:T(1,128)}, u32[]{:S(2)}, u32[]{:S(2)}) collective-permute-start(f32[1,3,6,1536]{3,0,2,1:T(1,128)} %stack.191), channel_id=1, source_target_pairs={{0,4},{4,8},{8,12},{12,16},{16,20},{20,24},{24,28},{1,5},{5,9},{9,... | collective-permute-start | bytes 331784 | tf_op jit(solution)/shard_map/ppermute | solution.py:25
  287.7 3.4 collective-permute-start.5
  291.4 7.4 collective-permute-start.7
  292.9 7.6 collective-permute-start.6
  437.8 12.0 collective-permute-start.8
  448.0 4.9 collective-permute-start.9
  453.2 7.9 collective-permute-start.11
  454.7 8.1 collective-permute-start.10
  467.4 66.4 %copy-start.25 = (f32[6,8192]{1,0:T(8,128)S(1)}, f32[6,8192]{1,0:T(8,128)}, u32[]{:S(2)}) copy-start(f32[6,8192]{1,0:T(8,128)} %copy-done.24) | copy-start | bytes 589828
  594.8 51.9 %collective-permute-start.12 = (f32[1,3,6,1536]{3,0,2,1:T(1,128)}, f32[1,3,6,1536]{3,0,2,1:T(1,128)}, u32[]{:S(2)}, u32[]{:S(2)}) collective-permute-start(f32[1,3,6,1536]{3,0,2,1:T(1,128)} %stack.209), channel_id=1, source_target_pairs={{0,4},{4,8},{8,12},{12,16},{16,20},{20,24},{24,28},{1,5},{5,9},{9,... | collective-permute-start | bytes 331784 | tf_op jit(solution)/shard_map/ppermute | solution.py:25
  644.8 3.4 collective-permute-start.13
  648.5 7.4 collective-permute-start.15
  650.0 7.6 collective-permute-start.14
  800.9 12.0 collective-permute-start.16
  811.1 4.9 collective-permute-start.17
  816.3 7.9 collective-permute-start.19
  817.8 8.1 collective-permute-start.18
  830.5 66.4 %copy-start.23 = (f32[6,8192]{1,0:T(8,128)S(1)}, f32[6,8192]{1,0:T(8,128)}, u32[]{:S(2)}) copy-start(f32[6,8192]{1,0:T(8,128)} %copy-done.22) | copy-start | bytes 589828
  957.3 51.9 %collective-permute-start.20 = (f32[1,3,6,1536]{3,0,2,1:T(1,128)S(1)}, f32[1,3,6,1536]{3,0,2,1:T(1,128)S(1)}, u32[]{:S(2)}, u32[]{:S(2)}) collective-permute-start(f32[1,3,6,1536]{3,0,2,1:T(1,128)S(1)} %stack.227), channel_id=1, source_target_pairs={{0,4},{4,8},{8,12},{12,16},{16,20},{20,24},{24,28},{1,5},{5,9},{9,... | collective-permute-start | bytes 331784 | tf_op jit(solution)/shard_map/ppermute | solution.py:25
  1007.3 3.2 collective-permute-start.21
  1010.8 7.4 collective-permute-start.23
  1012.3 7.6 collective-permute-start.22
  1154.4 11.5 collective-permute-start.24
  1164.0 5.1 collective-permute-start.25
  1169.4 7.9 collective-permute-start.27
  1170.9 8.1 collective-permute-start.26
  (88 other events, 767.4 us)
where the time goes:
time: 1270 us; the launch traced here: 1260 us
  other arithmetic  525 us (41%)
  local copies, waits for them, and re-layouts  487 us (38%)
  blocking collectives  127 us (10%)
  starting transfers between devices  82.6 us (7%)
  waiting for transfers between devices  25.6 us (2%)
    scatter-add x4, other arithmetic, spread(): accumulator[:, :bodies].at[:, flat_list]  254 us
    gather x3, local copies, waits for them, and re-layouts, shards(): gradient_outgoing = velocity[:, flat_list].reshape(6, 8, halo_width)  131 us
    psum x3, blocking collectives, shards(): lax.psum((partial_squares, partial_curve), ('bins', 'slab'))  127 us
    scatter-add x4, other arithmetic, spread(): accumulator = accumulator.at[:, second_body].add(second_terms)  112 us
    scatter-add x4, other arithmetic, spread(): accumulator = accumulator.at[:, first_body].add(first_terms)  109 us
    unnamed x251, local copies, waits for them, and re-layouts  72.1 us
    ppermute x14, starting transfers between devices, padded(): before = lax.ppermute(last, axis, up)  64 us
    gather x3, local copies, waits for them, and re-layouts, shards(): first_speed = extended[:, first_body]  53 us
  transfers between devices with their start and end apart: 28, of which 20 were waited for; matrix products, arithmetic and copies ran while one was open for 4% of the time, Pallas kernels for 0%

commit v1 on v0

v1 whole, which is shorter than its diff:
```python
import functools
import math

import jax
import jax.numpy as jnp
from jax import lax
from jax.experimental import pallas as pl
from jax.experimental.pallas import tpu as pltpu
from jax.sharding import PartitionSpec as P

ITERS = 3
SAFETY = 0.3
TINY = 1e-06
FLOOR = 1e-20
HI = 256
BF = jnp.bfloat16
F32 = jnp.float32
MESH = pl.DeviceIdType.MESH


def momentum_table(steps_count):
    theta_now = 1.0
    momentum = []
    for iteration in range(steps_count):
        theta_next = (
            -theta_now * theta_now + theta_now * math.sqrt(theta_now * theta_now + 4.0)
        ) / 2.0
        momentum.append(theta_now * (1.0 - theta_now) / (theta_now * theta_now + theta_next))
        theta_now = theta_next
    return momentum


def project(normal, tangent_one, tangent_two, friction):
    magnitude = jnp.sqrt(tangent_one * tangent_one + tangent_two * tangent_two)
    projected = jnp.maximum(friction * magnitude + normal, 0.0) / (friction * friction + 1.0)
    inside = magnitude <= friction * normal
    normal_new = jnp.where(inside, normal, projected)
    tangent_limit = friction * normal_new
    factor = tangent_limit / jnp.maximum(jnp.maximum(magnitude, tangent_limit), FLOOR)
    return normal_new, tangent_one * factor, tangent_two * factor


def split_rows(values):
    lead = values.astype(BF).astype(F32)
    return jnp.concatenate([lead, values - lead], axis=-2).astype(BF)


def chunk(index, width):
    return pl.ds(pl.multiple_of(index * width, width), width)


def kernel(
    n_bins, n_slab,
    fv_ref, im_ref, first_ref, second_ref, list_ref, jac_ref, bias_ref, comp_ref, fric_ref, warm_ref,
    imp_ref, vel_ref,
    hot, lo32, lo16, halo_hot, halo_lo32, halo_lo16,
    fvb, imb, x8, x16, acc, acc_halo, force, force_old, av, speed,
    point, point_old, gamma,
    out_f, out_v, in_f, in_v, part, sum_one, sum_two,
    send_f, recv_f, send_v, recv_v, send_one, recv_one, send_two, recv_two,
):
    bodies = fv_ref.shape[1]
    contacts = first_ref.shape[1]
    halo = list_ref.shape[1]
    n_lo = bodies // HI
    h_lo = halo // HI
    halo_los = 8 * h_lo
    ck = 512
    contacts_total = 3.0 * contacts * n_bins * n_slab
    b = lax.axis_index("bins")
    s = lax.axis_index("slab")

    def place(e):
        g = e + (e + 4) // 8
        return b + g // 3 - 1, s + g % 3 - 1

    def exists(e):
        nb, ns = place(e)
        return (nb >= 0) & (nb < n_bins) & (ns >= 0) & (ns < n_slab)

    def loop(count, body):
        def step(i, carry):
            body(i)
            return carry
        lax.fori_loop(0, count, step, 0)

    in_f[...] = jnp.zeros_like(in_f)
    in_v[...] = jnp.zeros_like(in_v)

    barrier = pltpu.get_barrier_semaphore()

    @functools.partial(loop, 8)
    def greet(e):
        @pl.when(exists(e))
        def _():
            pl.semaphore_signal(barrier, inc=1, device_id=place(e), device_id_type=MESH)

    @functools.partial(loop, n_slab - 1)
    def greet_slab(i):
        pl.semaphore_signal(barrier, inc=1, device_id=(b, (s + 1 + i) % n_slab), device_id_type=MESH)

    @functools.partial(loop, n_bins - 1)
    def greet_bins(i):
        pl.semaphore_signal(barrier, inc=1, device_id=((b + 1 + i) % n_bins, s), device_id_type=MESH)

    rows = lax.broadcasted_iota(jnp.int32, (HI, ck), 0)

    def index_parts(index, hot_to, lo32_to, lo16_to):
        low = jnp.broadcast_to(index // HI, (16, ck))
        hot_to[...] = jnp.where(rows == index % HI, 1.0, 0.0).astype(BF)
        lo32_to[...] = low[:8]
        lo16_to[...] = low.astype(F32).astype(BF)

    @functools.partial(loop, contacts // ck)
    def prepare(i):
        for half, ref in enumerate((first_ref, second_ref)):
            to = pl.ds(pl.multiple_of(half * contacts + i * ck, ck), ck)
            index_parts(ref[:, chunk(i, ck)], hot.at[:, to], lo32.at[:, to], lo16.at[:, to])

    for e in range(8):
        for c in range(halo // ck):
            to = pl.ds(c * ck, ck)
            index_parts(
                list_ref[e:e + 1, to],
                halo_hot.at[e, :, to], halo_lo32.at[e, :, to], halo_lo16.at[e, :, to],
            )

    fvb[...] = jnp.zeros_like(fvb)
    imb[...] = jnp.zeros_like(imb)
    for l in range(n_lo):
        fvb[l, 0:6, :] = fv_ref[:, l * HI:(l + 1) * HI]
        imb[l, 0:6, :] = im_ref[:, l * HI:(l + 1) * HI]
    x8[...] = jnp.zeros_like(x8)
    force_old[...] = jnp.zeros_like(force_old)
    point_old[...] = jnp.zeros_like(point_old)
    point[...] = warm_ref[...]
    gamma[...] = warm_ref[...]

    others = (n_slab - 1) + (n_bins - 1)
    up = jnp.where(b < n_bins - 1, 1, 0)
    down = jnp.where(b > 0, 1, 0)
    right = jnp.where(s < n_slab - 1, 1, 0)
    left = jnp.where(s > 0, 1, 0)
    pl.semaphore_wait(barrier, (1 + up + down) * (1 + left + right) - 1 + others)

    def copy(source, target, send, recv, e):
        return pltpu.make_async_remote_copy(
            src_ref=source.at[e], dst_ref=target.at[7 - e],
            send_sem=send.at[e], recv_sem=recv.at[7 - e],
            device_id=place(e), device_id_type=MESH,
        )

    def arrival(source, target, send, recv, e):
        return pltpu.make_async_remote_copy(
            src_ref=source.at[e], dst_ref=target.at[e],
            send_sem=send.at[e], recv_sem=recv.at[e],
            device_id=place(e), device_id_type=MESH,
        )

    def scatter(values, low, hot_part, first_lo, count):
        zero = jnp.zeros_like(values)
        tall = jnp.concatenate(
            [jnp.where(low == jnp.array(first_lo + l, BF), values, zero) for l in range(count)], axis=0
        )
        return lax.dot_general(tall, hot_part, (((1,), (1,)), ((), ())), preferred_element_type=F32)

    def gather(table, low, hot_part, first_lo, count):
        picked = jnp.dot(table, hot_part, preferred_element_type=F32)
        total = None
        for l in range(count):
            both = picked[l * 16:l * 16 + 8] + picked[l * 16 + 8:l * 16 + 16]
            both = jnp.where(low == first_lo + l, both, 0.0)
            total = both if total is None else total + both
        return total

    def spread(source):
        @functools.partial(loop, contacts // ck)
        def terms(i):
            at = chunk(i, ck)
            for half in range(2):
                x8[half, 0:6, :] = (
                    jac_ref[half, 0, :, at] * source[0:1, at]
                    + jac_ref[half, 1, :, at] * source[1:2, at]
                    + jac_ref[half, 2, :, at] * source[2:3, at]
                )
                x16[:, pl.ds(pl.multiple_of(half * contacts + i * ck, ck), ck)] = split_rows(x8[half])

        acc_halo[...] = jnp.zeros_like(acc_halo)

        @functools.partial(loop, contacts // ck)
        def halo_part(i):
            at = pl.ds(pl.multiple_of(contacts + i * ck, ck), ck)
            acc_halo[...] += scatter(x16[:, at], lo16[:, at], hot[:, at], n_lo, halo_los)

        for e in range(8):
            for m in range(h_lo):
                row = (e * h_lo + m) * 16
                out_f[e, :, m * HI:(m + 1) * HI] = acc_halo[row:row + 8] + acc_halo[row + 8:row + 16]

        @functools.partial(loop, 8)
        def send(e):
            @pl.when(exists(e))
            def _():
                copy(out_f, in_f, send_f, recv_f, e).start()

        acc[...] = jnp.zeros_like(acc)

        @functools.partial(loop, 2 * contacts // ck)
        def local_part(i):
            at = chunk(i, ck)
            acc[...] += scatter(x16[:, at], lo16[:, at], hot[:, at], 0, n_lo)

        @functools.partial(loop, 8)
        def arrived(e):
            @pl.when(exists(e))
            def _():
                arrival(out_f, in_f, send_f, recv_f, e).wait_recv()
            for c in range(halo // ck):
                at = pl.ds(c * ck, ck)
                acc[...] += scatter(
                    split_rows(in_f[e, :, at]), halo_lo16[e, :, at], halo_hot[e, :, at], 0, n_lo
                )

        both = acc[...].reshape(n_lo, 2, 8, HI)
        force[...] = both[:, 0] + both[:, 1]

        @functools.partial(loop, 8)
        def sent(e):
            @pl.when(exists(e))
            def _():
                copy(out_f, in_f, send_f, recv_f, e).wait_send()

    def lanes(values):
        row = jnp.sum(values, axis=0, keepdims=True)
        total = row[:, 0:128]
        for c in range(1, row.shape[1] // 128):
            total = total + row[:, c * 128:(c + 1) * 128]
        return total

    def slab_copy(k, i, slot):
        other = (s + 1 + i) % n_slab
        at = s if slot is None else slot
        return pltpu.make_async_remote_copy(
            src_ref=part.at[0], dst_ref=sum_one.at[k, at],
            send_sem=send_one.at[i], recv_sem=recv_one.at[k, at],
            device_id=(b, other), device_id_type=MESH,
        )

    def bins_copy(k, i, slot):
        other = (b + 1 + i) % n_bins
        at = b if slot is None else slot
        return pltpu.make_async_remote_copy(
            src_ref=part.at[1], dst_ref=sum_two.at[k, at],
            send_sem=send_two.at[i], recv_sem=recv_two.at[k, at],
            device_id=(other, s), device_id_type=MESH,
        )

    momentum = momentum_table(ITERS)

    def iteration(k):
        spread(point)

        change = point[...] - point_old[...]
        squares = change * change
        shift = force[...] - force_old[...]
        curve = (imb[...] * shift * shift).reshape(n_lo * 8, HI)
        part[0, 0:1, :] = lanes(squares)
        part[0, 1:2, :] = lanes(curve) + lanes(comp_ref[...] * squares)
        part[0, 2:8, :] = jnp.zeros((6, 128), F32)

        @functools.partial(loop, n_slab - 1)
        def send_slab(i):
            slab_copy(k, i, None).start()
        sum_one[k, s] = part[0]

        velocity = fvb[...] + imb[...] * force[...]
        av[0:n_lo * 16, :] = split_rows(velocity).reshape(n_lo * 16, HI)

        @functools.partial(loop, 8)
        def pull(e):
            for c in range(halo // ck):
                at = pl.ds(c * ck, ck)
                out_v[e, :, at] = gather(
                    av[0:n_lo * 16, :], halo_lo32[e, :, at], halo_hot[e, :, at], 0, n_lo
                )

            @pl.when(exists(e))
            def _():
                copy(out_v, in_v, send_v, recv_v, e).start()

        @functools.partial(loop, n_slab - 1)
        def wait_slab(i):
            slab_copy(k, i, (s + 1 + i) % n_slab).wait_recv()
        part[1] = functools.reduce(lambda x, y: x + y, [sum_one[k, i] for i in range(n_slab)])

        @functools.partial(loop, n_bins - 1)
        def send_bins(i):
            bins_copy(k, i, None).start()
        sum_two[k, b] = part[1]

        @functools.partial(loop, 2 * contacts // ck)
        def local_part(i):
            at = chunk(i, ck)
            speed[:, at] = gather(av[0:n_lo * 16, :], lo32[:, at], hot[:, at], 0, n_lo)

        @functools.partial(loop, n_bins - 1)
        def wait_bins(i):
            bins_copy(k, i, (b + 1 + i) % n_bins).wait_recv()
        total = functools.reduce(lambda x, y: x + y, [sum_two[k, i] for i in range(n_bins)])
        total = jnp.sum(total, axis=1, keepdims=True)
        step = (
            SAFETY * (total[0:1] / contacts_total + TINY) / (total[1:2] / contacts_total + TINY)
        )

        @functools.partial(loop, 8)
        def arrived(e):
            @pl.when(exists(e))
            def _():
                arrival(out_v, in_v, send_v, recv_v, e).wait_recv()
            for m in range(h_lo):
                row = pl.multiple_of((n_lo + e * h_lo + m) * 16, 16)
                av[pl.ds(row, 16), :] = split_rows(in_v[e, :, m * HI:(m + 1) * HI])

        beta = jnp.where(k == 0, momentum[0], jnp.where(k == 1, momentum[1], momentum[2])).astype(F32)

        @functools.partial(loop, contacts // ck)
        def update(i):
            at = chunk(i, ck)
            to = pl.ds(pl.multiple_of(contacts + i * ck, ck), ck)
            second = speed[:, to] + gather(
                av[n_lo * 16:, :], lo32[:, to], hot[:, to], n_lo, halo_los
            )
            second = second[0:6]
            first = speed[0:6, at]
            compliance = comp_ref[:, at]
            moved = []
            for r in range(3):
                here = point[r:r + 1, at]
                product = jac_ref[0, r, :, at] * first + jac_ref[1, r, :, at] * second
                slope = bias_ref[r:r + 1, at] + compliance * here + jnp.sum(product, axis=0, keepdims=True)
                moved.append(here - step * slope)
            updated = project(*moved, fric_ref[:, at])
            for r in range(3):
                point_old[r:r + 1, at] = point[r:r + 1, at]
                point[r:r + 1, at] = updated[r] + beta * (updated[r] - gamma[r:r + 1, at])
                gamma[r:r + 1, at] = updated[r]

        force_old[...] = force[...]

        @functools.partial(loop, 8)
        def sent(e):
            @pl.when(exists(e))
            def _():
                copy(out_v, in_v, send_v, recv_v, e).wait_send()

        @functools.partial(loop, n_slab - 1)
        def sent_slab(i):
            slab_copy(k, i, None).wait_send()

        @functools.partial(loop, n_bins - 1)
        def sent_bins(i):
            bins_copy(k, i, None).wait_send()

    loop(ITERS, iteration)
    spread(gamma)
    imp_ref[...] = gamma[...]
    for l in range(n_lo):
        vel_ref[:, l * HI:(l + 1) * HI] = (fvb[l] + imb[l] * force[l])[0:6]


def shards(
    n_bins, n_slab,
    free_velocity, inverse_mass, first_body, second_body, send_list,
    jacobian, contact_bias, compliance, friction, warm_start,
):
    bodies = free_velocity.shape[1]
    contacts = first_body.shape[0]
    halo = send_list.shape[1]
    n_lo = bodies // HI
    all_lo = n_lo + 8 * (halo // HI)
    dma = pltpu.SemaphoreType.DMA
    vm = pltpu.VMEM
    scratch = [
        vm((HI, 2 * contacts), BF), vm((8, 2 * contacts), jnp.int32), vm((16, 2 * contacts), BF),
        vm((8, HI, halo), BF), vm((8, 8, halo), jnp.int32), vm((8, 16, halo), BF),
        vm((n_lo, 8, HI), F32), vm((n_lo, 8, HI), F32), vm((2, 8, 512), F32), vm((16, 2 * contacts), BF),
        vm((n_lo * 16, HI), F32), vm(((all_lo - n_lo) * 16, HI), F32),
        vm((n_lo, 8, HI), F32), vm((n_lo, 8, HI), F32), vm((all_lo * 16, HI), BF), vm((8, 2 * contacts), F32),
        vm((3, contacts), F32), vm((3, contacts), F32), vm((3, contacts), F32),
        vm((8, 8, halo), F32), vm((8, 8, halo), F32), vm((8, 8, halo), F32), vm((8, 8, halo), F32),
        vm((2, 8, 128), F32), vm((ITERS, n_slab, 8, 128), F32), vm((ITERS, n_bins, 8, 128), F32),
        dma((8,)), dma((8,)), dma((8,)), dma((8,)),
        dma((n_slab,)), dma((ITERS, n_slab)), dma((n_bins,)), dma((ITERS, n_bins)),
    ]
    spec = pl.BlockSpec(memory_space=pltpu.VMEM)
    return pl.pallas_call(
        functools.partial(kernel, n_bins, n_slab),
        out_shape=(
            jax.ShapeDtypeStruct((3, contacts), F32),
            jax.ShapeDtypeStruct((6, bodies), F32),
        ),
        in_specs=[spec] * 10,
        out_specs=(spec, spec),
        scratch_shapes=scratch,
        compiler_params=pltpu.CompilerParams(
            collective_id=0, has_side_effects=True, vmem_limit_bytes=48 * 1024 * 1024
        ),
    )(
        free_velocity, inverse_mass, first_body[None], second_body[None], send_list,
        jacobian, contact_bias, compliance[None], friction[None], warm_start,
    )


def solution(mesh):
    return jax.shard_map(
        functools.partial(shards, mesh.shape["bins"], mesh.shape["slab"]),
        mesh=mesh,
        in_specs=(
            P(None, ("bins", "slab")),
            P(None, ("bins", "slab")),
            P(("bins", "slab")),
            P(("bins", "slab")),
            P(None, ("bins", "slab")),
            P(None, None, None, ("bins", "slab")),
            P(None, ("bins", "slab")),
            P(("bins", "slab")),
            P(("bins", "slab")),
            P(None, ("bins", "slab")),
        ),
        out_specs=(P(None, ("bins", "slab")), P(None, ("bins", "slab"))),
        check_vma=False,
    )
```

time: 1270 us -> 109 us (0.09)
  other arithmetic: 525 us -> 0 us
  local copies, waits for them, and re-layouts: 487 us -> 2.85 us
  blocking collectives: 127 us -> 0 us
  Pallas kernels: 0 us -> 105 us
  starting transfers between devices: 82.6 us -> 0 us
  waiting for transfers between devices: 25.6 us -> 0 us
    scatter-add x12 -> x0, other arithmetic: 476 us -> none  [the longest x4 254 us: spread(): accumulator[:, :bodies].at[:, flat_list]]
    gather x9 -> x0, local copies, waits for them, and re-layouts: 232 us -> none  [the longest x3 131 us: shards(): gradient_outgoing = velocity[:, flat_list].reshape(6, 8, halo_width)]
    psum x3 -> x0, blocking collectives: 127 us -> none  [shards(): lax.psum((partial_squares, partial_curve), ('bins', 'slab'))]
    slice x50 -> x0, local copies, waits for them, and re-layouts: 109 us -> none  [the longest x3 29.3 us: shards(): first_speed[column]]
    pallas_call x0 -> x1, Pallas kernels: none -> 105 us  [shards(): pl.pallas_call(functools.partial(kernel, n_bins, n_slab), out_shape=(jax....]
    ppermute x28 -> x0, starting transfers between devices: 82.6 us -> none  [the longest x14 64 us: padded(): before = lax.ppermute(last, axis, up)]
    unnamed x251 -> x21, local copies, waits for them, and re-layouts: 72.1 us -> 2.85 us
    concatenate x3 -> x0, other arithmetic: 31.8 us -> none  [shards(): jnp.concatenate([velocity, gradient_incoming.reshape(6, 8 * halo_width)],...]
  transfers between devices with their start and end apart: 28 -> 0, of which waited for: 20 -> 0; matrix products, arithmetic and copies ran while one was open for 4% -> 0% of each run, Pallas kernels for 0% -> 0%
where the time goes in v1:
time: 109 us
  Pallas kernels  105 us (96%)
  local copies, waits for them, and re-layouts  2.85 us (3%)
    pallas_call x1, Pallas kernels, shards(): pl.pallas_call(functools.partial(kernel, n_bins, n_slab), out_shape=(jax....  105 us
    unnamed x21, local copies, waits for them, and re-layouts  2.85 us

profile of v1, /device:TPU:0, one launch (start us, length us, event | category | flops | bytes accessed | tf_op | source)
XLA Modules:
  0.0 109.1 jit_solution(7173037817654256637)
XLA Ops:
  0.6 0.0 copy-start
  0.6 0.0 copy-start.1
  0.7 0.0 copy-start.2
  0.7 0.0 copy-start.3
  0.7 0.0 copy-start.4
  0.7 0.0 copy-start.5
  0.7 0.0 copy-start.6
  0.7 0.0 copy-start.7
  0.7 0.0 copy-start.8
  0.7 1.5 %copy.12.jac_ref = f32[2,3,6,4096]{3,2,1,0:T(8,128)S(1)} copy(f32[2,3,6,4096]{3,0,2,1:T(2,128)} %param.15) | data formatting | bytes 1179648 | tf_op args[5]
  2.2 0.0 copy-done
  2.2 0.0 copy-done.1
  2.2 0.0 copy-done.2
  2.2 0.0 copy-done.3
  2.2 0.0 copy-done.4
  2.2 0.0 copy-done.5
  2.3 0.0 copy-done.6
  2.3 0.0 copy-done.7
  2.3 0.0 copy-done.8
  2.3 105.5 %shard_map.113 = (f32[3,4096]{1,0:T(4,128)S(1)}, f32[6,8192]{1,0:T(8,128)S(1)}) custom-call(f32[6,8192]{1,0:T(8,128)S(1)} %copy-done, f32[6,8192]{1,0:T(8,128)S(1)} %copy-done.1, s32[1,4096]{1,0:T(1,128)S(1)} %bitcast.4, s32[1,4096]{1,0:T(1,128)S(1)} %bitcast.5, s32[8,1536]{1,0:T(8,128)S(1)} %copy-done.4, f32[2,3,6,4096]{3,2,1,0:T(8,128)S(1)} %copy.12.jac_ref, ...), custom_call_target="tpu_custom_call" | custom-call | tf_op jit(solution)/shard_map/pallas_call | solution.py:396
  107.8 0.6 copy.15
  108.4 0.7 copy.16
Async XLA Ops:
  0.6 1.6 %copy-start = (f32[6,8192]{1,0:T(8,128)S(1)}, f32[6,8192]{1,0:T(8,128)}, u32[]{:S(2)}) copy-start(f32[6,8192]{1,0:T(8,128)} %fv_ref.1) | copy-start | bytes 589828
  0.6 1.6 %copy-start.1 = (f32[6,8192]{1,0:T(8,128)S(1)}, f32[6,8192]{1,0:T(8,128)}, u32[]{:S(2)}) copy-start(f32[6,8192]{1,0:T(8,128)} %im_ref.1) | copy-start | bytes 589828
  0.7 1.6 %copy-start.2 = (f32[3,4096]{1,0:T(4,128)S(1)}, f32[3,4096]{1,0:T(4,128)}, u32[]{:S(2)}) copy-start(f32[3,4096]{1,0:T(4,128)} %bias_ref.1) | copy-start | bytes 147460
  0.7 1.6 %copy-start.3 = (f32[3,4096]{1,0:T(4,128)S(1)}, f32[3,4096]{1,0:T(4,128)}, u32[]{:S(2)}) copy-start(f32[3,4096]{1,0:T(4,128)} %warm_ref.1) | copy-start | bytes 147460
  0.7 1.6 %copy-start.4 = (s32[8,1536]{1,0:T(8,128)S(1)}, s32[8,1536]{1,0:T(8,128)}, u32[]{:S(2)}) copy-start(s32[8,1536]{1,0:T(8,128)} %list_ref.1) | copy-start | bytes 147460
  0.7 1.6 %copy-start.5 = (s32[4096]{0:T(1024)S(1)}, s32[4096]{0:T(1024)}, u32[]{:S(2)}) copy-start(s32[4096]{0:T(1024)} %param.12) | copy-start | bytes 49156
  0.7 1.6 %copy-start.6 = (s32[4096]{0:T(1024)S(1)}, s32[4096]{0:T(1024)}, u32[]{:S(2)}) copy-start(s32[4096]{0:T(1024)} %param.13) | copy-start | bytes 49156
  0.7 1.6 %copy-start.7 = (f32[4096]{0:T(1024)S(1)}, f32[4096]{0:T(1024)}, u32[]{:S(2)}) copy-start(f32[4096]{0:T(1024)} %param.17) | copy-start | bytes 49156
  0.7 1.6 %copy-start.8 = (f32[4096]{0:T(1024)S(1)}, f32[4096]{0:T(1024)}, u32[]{:S(2)}) copy-start(f32[4096]{0:T(1024)} %param.18) | copy-start | bytes 49156

commit v2 on v1

--- a/solution.py
+++ b/solution.py
@@ -40,9 +40,15 @@
     return normal_new, tangent_one * factor, tangent_two * factor
 
 
-def split_rows(values):
+def split(values):
     lead = values.astype(BF).astype(F32)
-    return jnp.concatenate([lead, values - lead], axis=-2).astype(BF)
+    return lead, values - lead
+
+
+def pack(values):
+    lead, rest = split(values)
+    twice = jnp.concatenate([lead, rest, lead, rest], axis=0)
+    return jnp.concatenate([twice, twice], axis=0).astype(BF)
 
 
 def chunk(index, width):
@@ -54,7 +60,7 @@
     fv_ref, im_ref, first_ref, second_ref, list_ref, jac_ref, bias_ref, comp_ref, fric_ref, warm_ref,
     imp_ref, vel_ref,
     hot, lo32, lo16, halo_hot, halo_lo32, halo_lo16,
-    fvb, imb, x8, x16, acc, acc_halo, force, force_old, av, speed,
+    fvb, imb, x48, acc, acc_halo, force, force_old, table, av, speed,
     point, point_old, gamma,
     out_f, out_v, in_f, in_v, part, sum_one, sum_two,
     send_f, recv_f, send_v, recv_v, send_one, recv_one, send_two, recv_two,
@@ -117,20 +123,23 @@
             to = pl.ds(pl.multiple_of(half * contacts + i * ck, ck), ck)
             index_parts(ref[:, chunk(i, ck)], hot.at[:, to], lo32.at[:, to], lo16.at[:, to])
 
-    for e in range(8):
-        for c in range(halo // ck):
-            to = pl.ds(c * ck, ck)
-            index_parts(
-                list_ref[e:e + 1, to],
-                halo_hot.at[e, :, to], halo_lo32.at[e, :, to], halo_lo16.at[e, :, to],
-            )
+    def prepare_halo():
+        for e in range(8):
+            for c in range(halo // ck):
+                to = pl.ds(c * ck, ck)
+                index_parts(
+                    list_ref[e:e + 1, to],
+                    halo_hot.at[e, :, to], halo_lo32.at[e, :, to], halo_lo16.at[e, :, to],
+                )
+        for l in range(n_lo):
+            fvb[l, 0:6, :] = fv_ref[:, l * HI:(l + 1) * HI]
+            imb[l, 0:6, :] = im_ref[:, l * HI:(l + 1) * HI]
 
     fvb[...] = jnp.zeros_like(fvb)
     imb[...] = jnp.zeros_like(imb)
-    for l in range(n_lo):
-        fvb[l, 0:6, :] = fv_ref[:, l * HI:(l + 1) * HI]
-        imb[l, 0:6, :] = im_ref[:, l * HI:(l + 1) * HI]
-    x8[...] = jnp.zeros_like(x8)
+    out_f[...] = jnp.zeros_like(out_f)
+    out_v[...] = jnp.zeros_like(out_v)
+    force[...] = jnp.zeros_like(force)
     force_old[...] = jnp.zeros_like(force_old)
     point_old[...] = jnp.zeros_like(point_old)
     point[...] = warm_ref[...]
@@ -158,44 +167,53 @@
         )
 
     def scatter(values, low, hot_part, first_lo, count):
-        zero = jnp.zeros_like(values)
-        tall = jnp.concatenate(
-            [jnp.where(low == jnp.array(first_lo + l, BF), values, zero) for l in range(count)], axis=0
-        )
+        tiles = [None] * (count * 12 // 16)
+        zero = jnp.zeros(low.shape, BF)
+        for t in range(3):
+            owner = (lax.broadcasted_iota(jnp.int32, low.shape, 0) + 16 * t) // 12
+            left_over = low - owner.astype(F32).astype(BF)
+            part_t = values[16 * t:16 * t + 16]
+            for j in range(count // 4):
+                tiles[3 * j + t] = jnp.where(left_over == jnp.array(first_lo + 4 * j, BF), part_t, zero)
+        tall = jnp.concatenate(tiles, axis=0)
         return lax.dot_general(tall, hot_part, (((1,), (1,)), ((), ())), preferred_element_type=F32)
 
-    def gather(table, low, hot_part, first_lo, count):
-        picked = jnp.dot(table, hot_part, preferred_element_type=F32)
-        total = None
-        for l in range(count):
-            both = picked[l * 16:l * 16 + 8] + picked[l * 16 + 8:l * 16 + 16]
-            both = jnp.where(low == first_lo + l, both, 0.0)
-            total = both if total is None else total + both
-        return total
-
-    def spread(source):
+    def gather(rows_of, low, hot_part, first_lo, count):
+        picked = jnp.dot(rows_of, hot_part, preferred_element_type=F32)
+        sums = []
+        for t in range(3):
+            left_over = low - (lax.broadcasted_iota(jnp.int32, low.shape, 0) + 8 * t) // 12
+            total = None
+            for j in range(count // 2):
+                row = (3 * j + t) * 8
+                term = jnp.where(left_over == first_lo + 2 * j, picked[row:row + 8], 0.0)
+                total = term if total is None else total + term
+            sums.append(total)
+        sums = jnp.concatenate(sums, axis=0)
+        return (sums[0:6] + sums[6:12]) + (sums[12:18] + sums[18:24])
+
+    def spread(meanwhile=None):
         @functools.partial(loop, contacts // ck)
         def terms(i):
             at = chunk(i, ck)
             for half in range(2):
-                x8[half, 0:6, :] = (
-                    jac_ref[half, 0, :, at] * source[0:1, at]
-                    + jac_ref[half, 1, :, at] * source[1:2, at]
-                    + jac_ref[half, 2, :, at] * source[2:3, at]
+                x48[:, pl.ds(pl.multiple_of(half * contacts + i * ck, ck), ck)] = pack(
+                    jac_ref[half, 0, :, at] * point[0:1, at]
+                    + jac_ref[half, 1, :, at] * point[1:2, at]
+                    + jac_ref[half, 2, :, at] * point[2:3, at]
                 )
-                x16[:, pl.ds(pl.multiple_of(half * contacts + i * ck, ck), ck)] = split_rows(x8[half])
 
         acc_halo[...] = jnp.zeros_like(acc_halo)
 
         @functools.partial(loop, contacts // ck)
         def halo_part(i):
             at = pl.ds(pl.multiple_of(contacts + i * ck, ck), ck)
-            acc_halo[...] += scatter(x16[:, at], lo16[:, at], hot[:, at], n_lo, halo_los)
+            acc_halo[...] += scatter(x48[:, at], lo16[:, at], hot[:, at], n_lo, halo_los)
 
         for e in range(8):
             for m in range(h_lo):
-                row = (e * h_lo + m) * 16
-                out_f[e, :, m * HI:(m + 1) * HI] = acc_halo[row:row + 8] + acc_halo[row + 8:row + 16]
+                row = (e * h_lo + m) * 12
+                out_f[e, 0:6, m * HI:(m + 1) * HI] = acc_halo[row:row + 6] + acc_halo[row + 6:row + 12]
 
         @functools.partial(loop, 8)
         def send(e):
@@ -203,12 +221,14 @@
             def _():
                 copy(out_f, in_f, send_f, recv_f, e).start()
 
+        if meanwhile is not None:
+            meanwhile()
         acc[...] = jnp.zeros_like(acc)
 
         @functools.partial(loop, 2 * contacts // ck)
         def local_part(i):
             at = chunk(i, ck)
-            acc[...] += scatter(x16[:, at], lo16[:, at], hot[:, at], 0, n_lo)
+            acc[...] += scatter(x48[:, at], lo16[:, at], hot[:, at], 0, n_lo)
 
         @functools.partial(loop, 8)
         def arrived(e):
@@ -218,11 +238,11 @@
             for c in range(halo // ck):
                 at = pl.ds(c * ck, ck)
                 acc[...] += scatter(
-                    split_rows(in_f[e, :, at]), halo_lo16[e, :, at], halo_hot[e, :, at], 0, n_lo
+                    pack(in_f[e, 0:6, at]), halo_lo16[e, :, at], halo_hot[e, :, at], 0, n_lo
                 )
 
-        both = acc[...].reshape(n_lo, 2, 8, HI)
-        force[...] = both[:, 0] + both[:, 1]
+        for l in range(n_lo):
+            force[l, 0:6, :] = acc[l * 12:l * 12 + 6] + acc[l * 12 + 6:l * 12 + 12]
 
         @functools.partial(loop, 8)
         def sent(e):
@@ -258,8 +278,6 @@
     momentum = momentum_table(ITERS)
 
     def iteration(k):
-        spread(point)
-
         change = point[...] - point_old[...]
         squares = change * change
         shift = force[...] - force_old[...]
@@ -273,15 +291,18 @@
             slab_copy(k, i, None).start()
         sum_one[k, s] = part[0]
 
-        velocity = fvb[...] + imb[...] * force[...]
-        av[0:n_lo * 16, :] = split_rows(velocity).reshape(n_lo * 16, HI)
+        for l in range(n_lo):
+            lead, rest = split(fvb[l, 0:6] + imb[l, 0:6] * force[l, 0:6])
+            table[l * 12:l * 12 + 6, :] = lead
+            table[l * 12 + 6:l * 12 + 12, :] = rest
+        av[0:n_lo * 12, :] = table[0:n_lo * 12, :].astype(BF)
 
         @functools.partial(loop, 8)
         def pull(e):
             for c in range(halo // ck):
                 at = pl.ds(c * ck, ck)
-                out_v[e, :, at] = gather(
-                    av[0:n_lo * 16, :], halo_lo32[e, :, at], halo_hot[e, :, at], 0, n_lo
+                out_v[e, 0:6, at] = gather(
+                    av[0:n_lo * 12, :], halo_lo32[e, :, at], halo_hot[e, :, at], 0, n_lo
                 )
 
             @pl.when(exists(e))
@@ -301,7 +322,7 @@
         @functools.partial(loop, 2 * contacts // ck)
         def local_part(i):
             at = chunk(i, ck)
-            speed[:, at] = gather(av[0:n_lo * 16, :], lo32[:, at], hot[:, at], 0, n_lo)
+            speed[0:6, at] = gather(av[0:n_lo * 12, :], lo32[:, at], hot[:, at], 0, n_lo)
 
         @functools.partial(loop, n_bins - 1)
         def wait_bins(i):
@@ -312,25 +333,28 @@
             SAFETY * (total[0:1] / contacts_total + TINY) / (total[1:2] / contacts_total + TINY)
         )
 
-        @functools.partial(loop, 8)
-        def arrived(e):
+        for e in range(8):
             @pl.when(exists(e))
             def _():
                 arrival(out_v, in_v, send_v, recv_v, e).wait_recv()
             for m in range(h_lo):
-                row = pl.multiple_of((n_lo + e * h_lo + m) * 16, 16)
-                av[pl.ds(row, 16), :] = split_rows(in_v[e, :, m * HI:(m + 1) * HI])
-
-        beta = jnp.where(k == 0, momentum[0], jnp.where(k == 1, momentum[1], momentum[2])).astype(F32)
+                row = (n_lo + e * h_lo + m) * 12
+                lead, rest = split(in_v[e, 0:6, m * HI:(m + 1) * HI])
+                table[row:row + 6, :] = lead
+                table[row + 6:row + 12, :] = rest
+        av[n_lo * 12:, :] = table[n_lo * 12:, :].astype(BF)
+
+        beta = jnp.float32(0.0)
+        for i in range(ITERS - 1):
+            beta = jnp.where(k == i, jnp.float32(momentum[i]), beta)
 
         @functools.partial(loop, contacts // ck)
         def update(i):
             at = chunk(i, ck)
             to = pl.ds(pl.multiple_of(contacts + i * ck, ck), ck)
-            second = speed[:, to] + gather(
-                av[n_lo * 16:, :], lo32[:, to], hot[:, to], n_lo, halo_los
+            second = speed[0:6, to] + gather(
+                av[n_lo * 12:, :], lo32[:, to], hot[:, to], n_lo, halo_los
             )
-            second = second[0:6]
             first = speed[0:6, at]
             compliance = comp_ref[:, at]
             moved = []
@@ -361,8 +385,10 @@
         def sent_bins(i):
             bins_copy(k, i, None).wait_send()
 
+        spread()
+
+    spread(prepare_halo)
     loop(ITERS, iteration)
-    spread(gamma)
     imp_ref[...] = gamma[...]
     for l in range(n_lo):
         vel_ref[:, l * HI:(l + 1) * HI] = (fvb[l] + imb[l] * force[l])[0:6]
@@ -383,9 +409,9 @@
     scratch = [
         vm((HI, 2 * contacts), BF), vm((8, 2 * contacts), jnp.int32), vm((16, 2 * contacts), BF),
         vm((8, HI, halo), BF), vm((8, 8, halo), jnp.int32), vm((8, 16, halo), BF),
-        vm((n_lo, 8, HI), F32), vm((n_lo, 8, HI), F32), vm((2, 8, 512), F32), vm((16, 2 * contacts), BF),
-        vm((n_lo * 16, HI), F32), vm(((all_lo - n_lo) * 16, HI), F32),
-        vm((n_lo, 8, HI), F32), vm((n_lo, 8, HI), F32), vm((all_lo * 16, HI), BF), vm((8, 2 * contacts), F32),
+        vm((n_lo, 8, HI), F32), vm((n_lo, 8, HI), F32), vm((48, 2 * contacts), BF),
+        vm((n_lo * 12, HI), F32), vm(((all_lo - n_lo) * 12, HI), F32),
+        vm((n_lo, 8, HI), F32), vm((n_lo, 8, HI), F32), vm((all_lo * 12, HI), F32), vm((all_lo * 12, HI), BF), vm((8, 2 * contacts), F32),
         vm((3, contacts), F32), vm((3, contacts), F32), vm((3, contacts), F32),
         vm((8, 8, halo), F32), vm((8, 8, halo), F32), vm((8, 8, halo), F32), vm((8, 8, halo), F32),
         vm((2, 8, 128), F32), vm((ITERS, n_slab, 8, 128), F32), vm((ITERS, n_bins, 8, 128), F32),

time: 109 us -> 99.6 us (0.914)
  Pallas kernels: 105 us -> 95.9 us
    pallas_call x1, Pallas kernels: 105 us -> 95.9 us  [shards(): pl.pallas_call(functools.partial(kernel, n_bins, n_slab), out_shape=(jax....]
where the time goes in v2:
time: 99.6 us; the launch traced here: 99.5 us
  Pallas kernels  95.9 us (96%)
  local copies, waits for them, and re-layouts  2.85 us (3%)
    pallas_call x1, Pallas kernels, shards(): pl.pallas_call(functools.partial(kernel, n_bins, n_slab), out_shape=(jax....  95.9 us
    unnamed x21, local copies, waits for them, and re-layouts  2.85 us

profile of v2, /device:TPU:0, one launch (start us, length us, event | category | flops | bytes accessed | tf_op | source)
XLA Modules:
  0.0 99.5 jit_solution(13607884828180771184)
XLA Ops:
  0.6 0.0 copy-start
  0.6 0.0 copy-start.1
  0.7 0.0 copy-start.2
  0.7 0.0 copy-start.3
  0.7 0.0 copy-start.4
  0.7 0.0 copy-start.5
  0.7 0.0 copy-start.6
  0.7 0.0 copy-start.7
  0.7 0.0 copy-start.8
  0.7 1.5 %copy.12.jac_ref = f32[2,3,6,4096]{3,2,1,0:T(8,128)S(1)} copy(f32[2,3,6,4096]{3,0,2,1:T(2,128)} %param.15) | data formatting | bytes 1179648 | tf_op args[5]
  2.2 0.0 copy-done
  2.2 0.0 copy-done.1
  2.2 0.0 copy-done.2
  2.2 0.0 copy-done.3
  2.2 0.0 copy-done.4
  2.2 0.0 copy-done.5
  2.3 0.0 copy-done.6
  2.3 0.0 copy-done.7
  2.3 0.0 copy-done.8
  2.3 95.9 %shard_map.113 = (f32[3,4096]{1,0:T(4,128)S(1)}, f32[6,8192]{1,0:T(8,128)S(1)}) custom-call(f32[6,8192]{1,0:T(8,128)S(1)} %copy-done, f32[6,8192]{1,0:T(8,128)S(1)} %copy-done.1, s32[1,4096]{1,0:T(1,128)S(1)} %bitcast.4, s32[1,4096]{1,0:T(1,128)S(1)} %bitcast.5, s32[8,1536]{1,0:T(8,128)S(1)} %copy-done.4, f32[2,3,6,4096]{3,2,1,0:T(8,128)S(1)} %copy.12.jac_ref, ...), custom_call_target="tpu_custom_call" | custom-call | tf_op jit(solution)/shard_map/pallas_call | solution.py:422
  98.2 0.6 copy.15
  98.8 0.7 copy.16
Async XLA Ops:
  0.6 1.6 %copy-start = (f32[6,8192]{1,0:T(8,128)S(1)}, f32[6,8192]{1,0:T(8,128)}, u32[]{:S(2)}) copy-start(f32[6,8192]{1,0:T(8,128)} %fv_ref.1) | copy-start | bytes 589828
  0.6 1.6 %copy-start.1 = (f32[6,8192]{1,0:T(8,128)S(1)}, f32[6,8192]{1,0:T(8,128)}, u32[]{:S(2)}) copy-start(f32[6,8192]{1,0:T(8,128)} %im_ref.1) | copy-start | bytes 589828
  0.7 1.6 %copy-start.2 = (f32[3,4096]{1,0:T(4,128)S(1)}, f32[3,4096]{1,0:T(4,128)}, u32[]{:S(2)}) copy-start(f32[3,4096]{1,0:T(4,128)} %bias_ref.1) | copy-start | bytes 147460
  0.7 1.6 %copy-start.3 = (f32[3,4096]{1,0:T(4,128)S(1)}, f32[3,4096]{1,0:T(4,128)}, u32[]{:S(2)}) copy-start(f32[3,4096]{1,0:T(4,128)} %warm_ref.1) | copy-start | bytes 147460
  0.7 1.6 %copy-start.4 = (s32[8,1536]{1,0:T(8,128)S(1)}, s32[8,1536]{1,0:T(8,128)}, u32[]{:S(2)}) copy-start(s32[8,1536]{1,0:T(8,128)} %list_ref.1) | copy-start | bytes 147460
  0.7 1.6 %copy-start.5 = (s32[4096]{0:T(1024)S(1)}, s32[4096]{0:T(1024)}, u32[]{:S(2)}) copy-start(s32[4096]{0:T(1024)} %param.12) | copy-start | bytes 49156
  0.7 1.6 %copy-start.6 = (s32[4096]{0:T(1024)S(1)}, s32[4096]{0:T(1024)}, u32[]{:S(2)}) copy-start(s32[4096]{0:T(1024)} %param.13) | copy-start | bytes 49156
  0.7 1.6 %copy-start.7 = (f32[4096]{0:T(1024)S(1)}, f32[4096]{0:T(1024)}, u32[]{:S(2)}) copy-start(f32[4096]{0:T(1024)} %param.17) | copy-start | bytes 49156
  0.7 1.6 %copy-start.8 = (f32[4096]{0:T(1024)S(1)}, f32[4096]{0:T(1024)}, u32[]{:S(2)}) copy-start(f32[4096]{0:T(1024)} %param.18) | copy-start | bytes 49156

commit v3 on v2

--- a/solution.py
+++ b/solution.py
@@ -57,9 +57,9 @@
 
 def kernel(
     n_bins, n_slab,
-    fv_ref, im_ref, first_ref, second_ref, list_ref, jac_ref, bias_ref, comp_ref, fric_ref, warm_ref,
+    fv_ref, im_ref, first_ref, second_ref, list_ref, jac_in, bias_ref, comp_ref, fric_ref, warm_ref,
     imp_ref, vel_ref,
-    hot, lo32, lo16, halo_hot, halo_lo32, halo_lo16,
+    jac_ref, jac_sem, hot, lo32, lo16, halo_hot, halo_lo32, halo_lo16,
     fvb, imb, x48, acc, acc_halo, force, force_old, table, av, speed,
     point, point_old, gamma,
     out_f, out_v, in_f, in_v, part, sum_one, sum_two,
@@ -72,6 +72,7 @@
     h_lo = halo // HI
     halo_los = 8 * h_lo
     ck = 512
+    wide = math.gcd(contacts, 2048)
     contacts_total = 3.0 * contacts * n_bins * n_slab
     b = lax.axis_index("bins")
     s = lax.axis_index("slab")
@@ -89,6 +90,9 @@
             body(i)
             return carry
         lax.fori_loop(0, count, step, 0)
+
+    jac_copy = pltpu.make_async_copy(jac_in, jac_ref, jac_sem)
+    jac_copy.start()
 
     in_f[...] = jnp.zeros_like(in_f)
     in_v[...] = jnp.zeros_like(in_v)
@@ -145,6 +149,7 @@
     point[...] = warm_ref[...]
     gamma[...] = warm_ref[...]
 
+    jac_copy.wait()
     others = (n_slab - 1) + (n_bins - 1)
     up = jnp.where(b < n_bins - 1, 1, 0)
     down = jnp.where(b > 0, 1, 0)
@@ -154,14 +159,14 @@
 
     def copy(source, target, send, recv, e):
         return pltpu.make_async_remote_copy(
-            src_ref=source.at[e], dst_ref=target.at[7 - e],
+            src_ref=source.at[e, 0:6], dst_ref=target.at[7 - e, 0:6],
             send_sem=send.at[e], recv_sem=recv.at[7 - e],
             device_id=place(e), device_id_type=MESH,
         )
 
     def arrival(source, target, send, recv, e):
         return pltpu.make_async_remote_copy(
-            src_ref=source.at[e], dst_ref=target.at[e],
+            src_ref=source.at[e, 0:6], dst_ref=target.at[e, 0:6],
             send_sem=send.at[e], recv_sem=recv.at[e],
             device_id=place(e), device_id_type=MESH,
         )
@@ -193,11 +198,11 @@
         return (sums[0:6] + sums[6:12]) + (sums[12:18] + sums[18:24])
 
     def spread(meanwhile=None):
-        @functools.partial(loop, contacts // ck)
+        @functools.partial(loop, contacts // wide)
         def terms(i):
-            at = chunk(i, ck)
+            at = chunk(i, wide)
             for half in range(2):
-                x48[:, pl.ds(pl.multiple_of(half * contacts + i * ck, ck), ck)] = pack(
+                x48[:, pl.ds(pl.multiple_of(half * contacts + i * wide, wide), wide)] = pack(
                     jac_ref[half, 0, :, at] * point[0:1, at]
                     + jac_ref[half, 1, :, at] * point[1:2, at]
                     + jac_ref[half, 2, :, at] * point[2:3, at]
@@ -205,9 +210,9 @@
 
         acc_halo[...] = jnp.zeros_like(acc_halo)
 
-        @functools.partial(loop, contacts // ck)
+        @functools.partial(loop, contacts // wide)
         def halo_part(i):
-            at = pl.ds(pl.multiple_of(contacts + i * ck, ck), ck)
+            at = pl.ds(pl.multiple_of(contacts + i * wide, wide), wide)
             acc_halo[...] += scatter(x48[:, at], lo16[:, at], hot[:, at], n_lo, halo_los)
 
         for e in range(8):
@@ -225,9 +230,9 @@
             meanwhile()
         acc[...] = jnp.zeros_like(acc)
 
-        @functools.partial(loop, 2 * contacts // ck)
+        @functools.partial(loop, 2 * contacts // wide)
         def local_part(i):
-            at = chunk(i, ck)
+            at = chunk(i, wide)
             acc[...] += scatter(x48[:, at], lo16[:, at], hot[:, at], 0, n_lo)
 
         @functools.partial(loop, 8)
@@ -319,9 +324,9 @@
             bins_copy(k, i, None).start()
         sum_two[k, b] = part[1]
 
-        @functools.partial(loop, 2 * contacts // ck)
+        @functools.partial(loop, 2 * contacts // wide)
         def local_part(i):
-            at = chunk(i, ck)
+            at = chunk(i, wide)
             speed[0:6, at] = gather(av[0:n_lo * 12, :], lo32[:, at], hot[:, at], 0, n_lo)
 
         @functools.partial(loop, n_bins - 1)
@@ -348,10 +353,10 @@
         for i in range(ITERS - 1):
             beta = jnp.where(k == i, jnp.float32(momentum[i]), beta)
 
-        @functools.partial(loop, contacts // ck)
+        @functools.partial(loop, contacts // wide)
         def update(i):
-            at = chunk(i, ck)
-            to = pl.ds(pl.multiple_of(contacts + i * ck, ck), ck)
+            at = chunk(i, wide)
+            to = pl.ds(pl.multiple_of(contacts + i * wide, wide), wide)
             second = speed[0:6, to] + gather(
                 av[n_lo * 12:, :], lo32[:, to], hot[:, to], n_lo, halo_los
             )
@@ -407,6 +412,7 @@
     dma = pltpu.SemaphoreType.DMA
     vm = pltpu.VMEM
     scratch = [
+        vm((2, 3, 6, contacts), F32), dma,
         vm((HI, 2 * contacts), BF), vm((8, 2 * contacts), jnp.int32), vm((16, 2 * contacts), BF),
         vm((8, HI, halo), BF), vm((8, 8, halo), jnp.int32), vm((8, 16, halo), BF),
         vm((n_lo, 8, HI), F32), vm((n_lo, 8, HI), F32), vm((48, 2 * contacts), BF),
@@ -425,7 +431,7 @@
             jax.ShapeDtypeStruct((3, contacts), F32),
             jax.ShapeDtypeStruct((6, bodies), F32),
         ),
-        in_specs=[spec] * 10,
+        in_specs=[spec] * 5 + [pl.BlockSpec(memory_space=pl.ANY)] + [spec] * 4,
         out_specs=(spec, spec),
         scratch_shapes=scratch,
         compiler_params=pltpu.CompilerParams(

time: 99.6 us -> 81.1 us (0.81)
  Pallas kernels: 95.9 us -> 77.1 us
    pallas_call x1, Pallas kernels: 95.9 us -> 77.1 us  [shards(): pl.pallas_call(functools.partial(kernel, n_bins, n_slab), out_shape=(jax....]
where the time goes in v3:
time: 81.1 us; the launch traced here: 80.7 us
  Pallas kernels  77.1 us (95%)
  local copies, waits for them, and re-layouts  2.85 us (4%)
    pallas_call x1, Pallas kernels, shards(): pl.pallas_call(functools.partial(kernel, n_bins, n_slab), out_shape=(jax....  77.1 us
    unnamed x21, local copies, waits for them, and re-layouts  2.85 us

profile of v3, /device:TPU:0, one launch (start us, length us, event | category | flops | bytes accessed | tf_op | source)
XLA Modules:
  0.0 80.7 jit_solution(14127247001092441872)
XLA Ops:
  0.6 0.0 copy-start
  0.6 0.0 copy-start.1
  0.7 0.0 copy-start.2
  0.7 0.0 copy-start.3
  0.7 0.0 copy-start.4
  0.7 0.0 copy-start.5
  0.7 0.0 copy-start.6
  0.7 0.0 copy-start.7
  0.7 0.0 copy-start.8
  0.7 1.5 %copy.12.jac_in = f32[2,3,6,4096]{3,2,1,0:T(8,128)S(1)} copy(f32[2,3,6,4096]{3,0,2,1:T(2,128)} %param.15) | data formatting | bytes 1179648 | tf_op args[5]
  2.2 0.0 copy-done
  2.2 0.0 copy-done.1
  2.2 0.0 copy-done.2
  2.2 0.0 copy-done.3
  2.2 0.0 copy-done.4
  2.2 0.0 copy-done.5
  2.3 0.0 copy-done.6
  2.3 0.0 copy-done.7
  2.3 0.0 copy-done.8
  2.3 77.1 %shard_map.113 = (f32[3,4096]{1,0:T(4,128)S(1)}, f32[6,8192]{1,0:T(8,128)S(1)}) custom-call(f32[6,8192]{1,0:T(8,128)S(1)} %copy-done, f32[6,8192]{1,0:T(8,128)S(1)} %copy-done.1, s32[1,4096]{1,0:T(1,128)S(1)} %bitcast.4, s32[1,4096]{1,0:T(1,128)S(1)} %bitcast.5, s32[8,1536]{1,0:T(8,128)S(1)} %copy-done.4, f32[2,3,6,4096]{3,2,1,0:T(8,128)S(1)} %copy.12.jac_in, ...), custom_call_target="tpu_custom_call" | custom-call | tf_op jit(solution)/shard_map/pallas_call | solution.py:428
  79.4 0.6 copy.15
  80.0 0.7 copy.16
Async XLA Ops:
  0.6 1.6 %copy-start = (f32[6,8192]{1,0:T(8,128)S(1)}, f32[6,8192]{1,0:T(8,128)}, u32[]{:S(2)}) copy-start(f32[6,8192]{1,0:T(8,128)} %fv_ref.1) | copy-start | bytes 589828
  0.6 1.6 %copy-start.1 = (f32[6,8192]{1,0:T(8,128)S(1)}, f32[6,8192]{1,0:T(8,128)}, u32[]{:S(2)}) copy-start(f32[6,8192]{1,0:T(8,128)} %im_ref.1) | copy-start | bytes 589828
  0.7 1.6 %copy-start.2 = (f32[3,4096]{1,0:T(4,128)S(1)}, f32[3,4096]{1,0:T(4,128)}, u32[]{:S(2)}) copy-start(f32[3,4096]{1,0:T(4,128)} %bias_ref.1) | copy-start | bytes 147460
  0.7 1.6 %copy-start.3 = (f32[3,4096]{1,0:T(4,128)S(1)}, f32[3,4096]{1,0:T(4,128)}, u32[]{:S(2)}) copy-start(f32[3,4096]{1,0:T(4,128)} %warm_ref.1) | copy-start | bytes 147460
  0.7 1.6 %copy-start.4 = (s32[8,1536]{1,0:T(8,128)S(1)}, s32[8,1536]{1,0:T(8,128)}, u32[]{:S(2)}) copy-start(s32[8,1536]{1,0:T(8,128)} %list_ref.1) | copy-start | bytes 147460
  0.7 1.6 %copy-start.5 = (s32[4096]{0:T(1024)S(1)}, s32[4096]{0:T(1024)}, u32[]{:S(2)}) copy-start(s32[4096]{0:T(1024)} %param.12) | copy-start | bytes 49156
  0.7 1.6 %copy-start.6 = (s32[4096]{0:T(1024)S(1)}, s32[4096]{0:T(1024)}, u32[]{:S(2)}) copy-start(s32[4096]{0:T(1024)} %param.13) | copy-start | bytes 49156
  0.7 1.6 %copy-start.7 = (f32[4096]{0:T(1024)S(1)}, f32[4096]{0:T(1024)}, u32[]{:S(2)}) copy-start(f32[4096]{0:T(1024)} %param.17) | copy-start | bytes 49156
  0.7 1.6 %copy-start.8 = (f32[4096]{0:T(1024)S(1)}, f32[4096]{0:T(1024)}, u32[]{:S(2)}) copy-start(f32[4096]{0:T(1024)} %param.18) | copy-start | bytes 49156
